TPU v7x, 256 devices: a whole 4x4x8 slice. The times are simulated.
256 devices in a mesh: row: 16 (over z_hi, y), col: 16 (over z_lo, x, core).
Axes of the slice: x: 4, y: 4, z: 8 (z_hi: 4, z_lo: 2; z = z_hi * 2 + z_lo), core: 2. Of those that a mesh axis runs over, the one named last changes fastest.
Arguments:
- iterate: bfloat16 [7168, 10240], P('row', 'col'), may hold values from -0.03125 to 0.03125
Outputs:
- update: bfloat16 [7168, 10240], P('row', 'col')
All inputs are finite; a program needn't handle non-finite values.
Results may differ from a plain program's by a relative error of at most 0.017.
Values may be sent and summed in bfloat16 or wider, within the bound.
A program may use at most 128 MiB of HBM per device.

v0:
```python
import math

import jax
import jax.numpy as jnp
from jax import lax
from jax.sharding import PartitionSpec as P

N = 10240


def contract_first(left, right):
    return lax.dot_general(
        left, right, (((0,), (0,)), ((), ())), preferred_element_type=jnp.float32
    )


def contract_last(left, right):
    return lax.dot_general(
        left, right, (((1,), (1,)), ((), ())), preferred_element_type=jnp.float32
    )


def local(iterate):
    column = lax.all_gather(iterate, "row", axis=0, tiled=True)
    summed = lax.psum_scatter(
        contract_last(column, iterate).astype(jnp.bfloat16), "col", scatter_dimension=0, tiled=True
    )
    band_t = lax.all_gather(summed, "col", axis=0, tiled=True)
    applied = contract_first(band_t, column)
    applied_round = applied.astype(jnp.bfloat16)
    twice = contract_first(band_t, lax.all_gather(applied_round, "row", axis=0, tiled=True))
    total = 3.4445 * iterate.astype(jnp.float32) - 4.775 * applied + 2.0315 * twice
    return (math.sqrt(N) * total).astype(jnp.bfloat16)


def solution(mesh):
    in_specs = (P("row", "col"),)
    out_specs = P("row", "col")
    return jax.shard_map(local, mesh=mesh, in_specs=in_specs, out_specs=out_specs, check_vma=False)
```

profile of v0, /device:TPU:1, one launch (start us, length us, event | category | flops | bytes accessed | tf_op | source)
XLA Modules:
  0.0 420.5 jit_solution(12230230041782647856)
XLA Ops:
  6.5 0.0 all-gather.4.cloned.1.call-start
  6.5 0.7 all-gather.4.cloned.1.call-update
  7.3 0.0 reduce-scatter.2.cloned.1.call-start
  7.3 123.6 %all-gather.4.cloned.1.call-done = bf16[7168,640]{1,0:T(8,128)(2,1)} async-done(((bf16[448,640]{1,0:T(8,128)(2,1)}), bf16[7168,640]{1,0:T(8,128)(2,1)}) %all-gather.4.cloned.1.call-update) | async-done | bytes 9175056 | tf_op jit(solution)/shard_map/all_gather | solution.py:24
  130.9 10.4 %convolution_convert_fusion = bf16[7168,448]{1,0:T(8,128)(2,1)} fusion(bf16[7168,640]{1,0:T(8,128)(2,1)} %all-gather.4.cloned.1.call-done, bf16[448,640]{1,0:T(8,128)(2,1)} %param.1), kind=kOutput, calls=%fused_computation | convolution fusion | flops 4113629184 | bytes 16171008 | tf_op jit(solution)/shard_map/dot_general | solution.py:18
  141.3 0.0 reduce-scatter.2.cloned.1.call-update
  141.3 0.0 all-gather.6.cloned.1.call-start
  141.4 77.4 %reduce-scatter.2.cloned.1.call-done = bf16[448,448]{1,0:T(8,128)(2,1)} async-done(((bf16[7168,448]{1,0:T(8,128)(2,1)}), bf16[448,448]{1,0:T(8,128)(2,1)}) %reduce-scatter.2.cloned.1.call-update) | async-done | bytes 401424 | tf_op jit(solution)/shard_map/reduce_scatter | solution.py:25
  218.8 0.0 all-gather.6.cloned.1.call-update
  218.8 0.0 copy-start
  218.8 0.2 all-gather.8.cloned.1.call-start
  219.1 53.5 %all-gather.6.cloned.1.call-done = bf16[7168,448]{1,0:T(8,128)(2,1)} async-done(((bf16[448,448]{1,0:T(8,128)(2,1)}), bf16[7168,448]{1,0:T(8,128)(2,1)}) %all-gather.6.cloned.1.call-update) | async-done | bytes 6422544 | tf_op jit(solution)/shard_map/all_gather | solution.py:28
  272.6 11.7 %fusion.3 = (bf16[448,640]{1,0:T(8,128)(2,1)}, f32[448,640]{1,0:T(8,128)S(1)}) fusion(bf16[7168,448]{1,0:T(8,128)(2,1)} %all-gather.6.cloned.1.call-done, bf16[7168,640]{1,0:T(8,128)(2,1)} %all-gather.4.cloned.1.call-done), kind=kOutput, calls=%fused_computation.5 | convolution fusion | flops 4110704640 | bytes 17317888 | tf_op jit(solution)/shard_map/dot_general | solution.py:12
  284.2 0.0 all-gather.8.cloned.1.call-update
  284.3 117.9 %all-gather.8.cloned.1.call-done = bf16[7168,640]{1,0:T(8,128)(2,1)} async-done(((bf16[448,640]{1,0:T(8,128)(2,1)}), bf16[7168,640]{1,0:T(8,128)(2,1)}) %all-gather.8.cloned.1.call-update) | async-done | bytes 9175056 | tf_op jit(solution)/shard_map/all_gather | solution.py:31
  402.2 0.0 copy-done
  402.2 11.7 %fusion.2 = bf16[448,640]{1,0:T(8,128)(2,1)} fusion(bf16[7168,448]{1,0:T(8,128)(2,1)} %all-gather.6.cloned.1.call-done, bf16[7168,640]{1,0:T(8,128)(2,1)} %all-gather.8.cloned.1.call-done, f32[448,640]{1,0:T(8,128)S(1)} %get-tuple-element.6, bf16[448,640]{1,0:T(8,128)(2,1)S(1)} %copy-done), kind=kOutput, calls=%fused_computation.4 | convolution fusion | flops 4112711680 | bytes 17891328 | tf_op jit(solution)/shard_map/dot_general | solution.py:12
Async XLA Ops:
  6.5 124.4 %all-gather.4.cloned.1.call-start = ((), (), s32[]{:S(2)}) async-start(), calls=%async_computation.1 | async-start | bytes 9748480 | tf_op jit(solution)/shard_map/all_gather | solution.py:24
  7.3 211.5 %reduce-scatter.2.cloned.1.call-start = ((), (), s32[]{:S(2)}) async-start(), calls=%async_computation.2 | async-start | bytes 7798784 | tf_op jit(solution)/shard_map/reduce_scatter | solution.py:25
  141.3 131.2 %all-gather.6.cloned.1.call-start = ((), (), s32[]{:S(2)}) async-start(), calls=%async_computation.3 | async-start | bytes 7798784 | tf_op jit(solution)/shard_map/all_gather | solution.py:28
  218.8 183.4 %copy-start = (bf16[448,640]{1,0:T(8,128)(2,1)S(1)}, bf16[448,640]{1,0:T(8,128)(2,1)}, u32[]{:S(2)}) copy-start(bf16[448,640]{1,0:T(8,128)(2,1)} %param.1) | copy-start | bytes 1720324
  218.8 183.3 %all-gather.8.cloned.1.call-start = ((), (), s32[]{:S(2)}) async-start(), calls=%async_computation.4 | async-start | bytes 9748480 | tf_op jit(solution)/shard_map/all_gather | solution.py:31
Sparse Core Ops, SparseCore 0:
  9.8 121.1 all-gather.3
  141.5 77.2 reduce-scatter.1
  220.7 51.8 all-gather.5
  284.4 117.7 all-gather.7
where the time goes:
time: 427 us; the launch traced here: 420 us
  waiting for transfers between devices  373 us (87%)
  matrix products  33.8 us (8%)
  between operations  13.1 us (3%)
    all_gather x1, waiting for transfers between devices, local(): column = lax.all_gather(iterate, 'row', axis=0, tiled=True)  124 us
    all_gather x1, waiting for transfers between devices, local(): lax.all_gather(applied_round, 'row', axis=0, tiled=True)  118 us
    reduce_scatter x1, waiting for transfers between devices, local(): lax.psum_scatter(contract_last(column, iterate).astype(jnp.bfloat16), 'co...  77.4 us
    all_gather x1, waiting for transfers between devices, local(): band_t = lax.all_gather(summed, 'col', axis=0, tiled=True)  53.5 us
    dot_general x2, matrix products, contract_first(): lax.dot_general(left, right, (((0,), (0,)), ((), ())), preferred_element_...  23.4 us
    dot_general x1, matrix products, contract_last(): lax.dot_general(left, right, (((1,), (1,)), ((), ())), preferred_element_...  10.4 us
  transfers between devices with their start and end apart: 4, of which 4 were waited for; matrix products, arithmetic and copies ran while one was open for 0% of the time, Pallas kernels for 0%

commit v1 on v0

v1 whole, which is shorter than its diff:
```python
import math

import jax
import jax.numpy as jnp
from jax import lax
from jax.sharding import Mesh, PartitionSpec as P

N = 10240
F32 = jnp.float32
BF16 = jnp.bfloat16


def local(iterate):
    rows_i = lax.all_gather(iterate, "y", axis=0, tiled=True)
    rows_j = lax.all_gather(iterate, "zh", axis=0, tiled=True)
    part = lax.dot_general(
        rows_i, rows_j, (((1,), (1,)), ((), ())), preferred_element_type=F32
    ).astype(BF16)
    piece = lax.psum_scatter(part, ("zl", "x", "core"), scatter_dimension=0, tiled=True)
    gram = lax.all_gather(piece, ("zl", "x", "core"), axis=0, tiled=True)

    def apply(right):
        out = jnp.dot(gram, right, preferred_element_type=F32).astype(BF16)
        return lax.psum_scatter(out, "y", scatter_dimension=0, tiled=True)

    applied = apply(rows_j)
    twice = apply(lax.all_gather(applied, "zh", axis=0, tiled=True))
    total = (
        3.4445 * iterate.astype(F32)
        - 4.775 * applied.astype(F32)
        + 2.0315 * twice.astype(F32)
    )
    return (math.sqrt(N) * total).astype(BF16)


def solution(mesh):
    fine = Mesh(mesh.devices.reshape(4, 4, 2, 4, 2), ("zh", "y", "zl", "x", "core"))
    spec = P(("zh", "y"), ("zl", "x", "core"))
    return jax.shard_map(local, mesh=fine, in_specs=(spec,), out_specs=spec, check_vma=False)
```

time: 427 us -> 382 us (0.89); the launches traced: 420 us -> 381 us
  waiting for transfers between devices: 373 us -> 339 us
  matrix products: 33.8 us -> 26.5 us
    all_gather x3 -> x4, waiting for transfers between devices: 295 us -> 200 us  [the longest x1 55.7 us: local(): rows_j = lax.all_gather(iterate, 'zh', axis=0, tiled=True)]
    reduce_scatter x1 -> x3, waiting for transfers between devices: 77.4 us -> 137 us  [the longest x1 69.3 us: local(): lax.psum_scatter(part, ('zl', 'x', 'core'), scatter_dimension=0, tiled=True)]
    dot_general x3, matrix products: 33.8 us -> 26.5 us  [the longest x2 17.4 us: apply(): out = jnp.dot(gram, right, preferred_element_type=F32).astype(BF16)]
  transfers between devices with their start and end apart: 4 -> 7, of which waited for: 4 -> 7; matrix products, arithmetic and copies ran while one was open for 0% -> 0% of each run, Pallas kernels for 0% -> 0%
where the time goes in v1:
time: 382 us; the launch traced here: 381 us
  waiting for transfers between devices  339 us (89%)
  matrix products  26.5 us (7%)
  between operations  13.5 us (4%)
    reduce_scatter x1, waiting for transfers between devices, local(): lax.psum_scatter(part, ('zl', 'x', 'core'), scatter_dimension=0, tiled=True)  69.3 us
    reduce_scatter x2, waiting for transfers between devices, apply(): return lax.psum_scatter(out, 'y', scatter_dimension=0, tiled=True)  67.9 us
    all_gather x1, waiting for transfers between devices, local(): rows_j = lax.all_gather(iterate, 'zh', axis=0, tiled=True)  55.7 us
    all_gather x1, waiting for transfers between devices, local(): twice = apply(lax.all_gather(applied, 'zh', axis=0, tiled=True))  55.3 us
    all_gather x1, waiting for transfers between devices, local(): gram = lax.all_gather(piece, ('zl', 'x', 'core'), axis=0, tiled=True)  49.3 us
    all_gather x1, waiting for transfers between devices, local(): rows_i = lax.all_gather(iterate, 'y', axis=0, tiled=True)  40 us
    dot_general x2, matrix products, apply(): out = jnp.dot(gram, right, preferred_element_type=F32).astype(BF16)  17.4 us
    dot_general x1, matrix products, local(): lax.dot_general(rows_i, rows_j, (((1,), (1,)), ((), ())), preferred_eleme...  9.08 us
  transfers between devices with their start and end apart: 7, of which 7 were waited for; matrix products, arithmetic and copies ran while one was open for 0% of the time, Pallas kernels for 0%

profile of v1, /device:TPU:1, one launch (start us, length us, event | category | flops | bytes accessed | tf_op | source)
XLA Modules:
  0.0 381.4 jit_solution(15740430108308235526)
XLA Ops:
  6.5 0.0 all-gather.5.cloned.1.call-start
  6.5 0.7 all-gather.5.cloned.1.call-update
  7.3 0.0 all-gather.7.cloned.1.call-start
  7.3 0.7 all-gather.7.cloned.1.call-update
  8.0 0.0 reduce-scatter.4.cloned.1.call-start
  8.1 40.0 %all-gather.5.cloned.1.call-done = bf16[1792,640]{1,0:T(8,128)(2,1)} async-done(((bf16[448,640]{1,0:T(8,128)(2,1)}), bf16[1792,640]{1,0:T(8,128)(2,1)}) %all-gather.5.cloned.1.call-update) | async-done | bytes 2293776 | tf_op jit(solution)/shard_map/all_gather | solution.py:14
  48.0 55.7 %all-gather.7.cloned.1.call-done = bf16[1792,640]{1,0:T(8,128)(2,1)} async-done(((bf16[448,640]{1,0:T(8,128)(2,1)}), bf16[1792,640]{1,0:T(8,128)(2,1)}) %all-gather.7.cloned.1.call-update) | async-done | bytes 2293776 | tf_op jit(solution)/shard_map/all_gather | solution.py:15
  103.8 9.1 %convolution_convert_fusion = bf16[1792,1792]{1,0:T(8,128)(2,1)} fusion(bf16[1792,640]{1,0:T(8,128)(2,1)} %all-gather.5.cloned.1.call-done, bf16[1792,640]{1,0:T(8,128)(2,1)} %all-gather.7.cloned.1.call-done), kind=kOutput, calls=%fused_computation | convolution fusion | flops 4113629184 | bytes 11010048 | tf_op jit(solution)/shard_map/dot_general | solution.py:16
  112.8 0.0 copy-start.2
  112.8 0.0 reduce-scatter.4.cloned.1.call-update
  112.9 0.0 all-gather.9.cloned.1.call-start
  112.9 69.3 %reduce-scatter.4.cloned.1.call-done = bf16[112,1792]{1,0:T(8,128)(2,1)} async-done(((bf16[1792,1792]{1,0:T(8,128)(2,1)}), bf16[112,1792]{1,0:T(8,128)(2,1)}) %reduce-scatter.4.cloned.1.call-update) | async-done | bytes 401424 | tf_op jit(solution)/shard_map/reduce_scatter | solution.py:19
  182.2 0.0 all-gather.9.cloned.1.call-update
  182.2 0.0 reduce-scatter.6.cloned.1.call-start
  182.3 49.3 %all-gather.9.cloned.1.call-done = bf16[1792,1792]{1,0:T(8,128)(2,1)} async-done(((bf16[112,1792]{1,0:T(8,128)(2,1)}), bf16[1792,1792]{1,0:T(8,128)(2,1)}) %all-gather.9.cloned.1.call-update) | async-done | bytes 6422544 | tf_op jit(solution)/shard_map/all_gather | solution.py:20
  231.6 0.0 copy-done.2
  231.6 8.3 %convolution_convert_fusion.2 = bf16[1792,640]{1,0:T(8,128)(2,1)} fusion(bf16[1792,1792]{1,0:T(8,128)(2,1)} %all-gather.9.cloned.1.call-done, bf16[1792,640]{1,0:T(8,128)(2,1)S(1)} %copy-done.2), kind=kOutput, calls=%fused_computation.2 | convolution fusion | flops 4111564800 | bytes 11010048 | tf_op jit(solution)/shard_map/dot_general | solution.py:23
  239.9 0.0 reduce-scatter.6.cloned.1.call-update
  239.9 0.0 all-gather.11.cloned.1.call-start
  240.0 34.5 %reduce-scatter.6.cloned.1.call-done = bf16[448,640]{1,0:T(8,128)(2,1)} async-done(((bf16[1792,640]{1,0:T(8,128)(2,1)}), bf16[448,640]{1,0:T(8,128)(2,1)}) %reduce-scatter.6.cloned.1.call-update) | async-done | bytes 573456 | tf_op jit(solution)/shard_map/reduce_scatter | solution.py:24
  274.4 0.0 all-gather.11.cloned.1.call-update
  274.5 0.0 reduce-scatter.8.cloned.1.call-start
  274.5 55.3 %all-gather.11.cloned.1.call-done = bf16[1792,640]{1,0:T(8,128)(2,1)} async-done(((bf16[448,640]{1,0:T(8,128)(2,1)}), bf16[1792,640]{1,0:T(8,128)(2,1)}) %all-gather.11.cloned.1.call-update) | async-done | bytes 2293776 | tf_op jit(solution)/shard_map/all_gather | solution.py:27
  329.8 9.0 %convolution_convert_fusion.1 = bf16[1792,640]{1,0:T(8,128)(2,1)} fusion(bf16[1792,1792]{1,0:T(8,128)(2,1)} %all-gather.9.cloned.1.call-done, bf16[1792,640]{1,0:T(8,128)(2,1)} %all-gather.11.cloned.1.call-done), kind=kOutput, calls=%fused_computation.1 | convolution fusion | flops 4111564800 | bytes 11010048 | tf_op jit(solution)/shard_map/dot_general | solution.py:23
  338.8 0.0 copy-start
  338.8 0.0 copy-start.1
  338.8 0.0 reduce-scatter.8.cloned.1.call-update
  338.8 33.5 %reduce-scatter.8.cloned.1.call-done = bf16[448,640]{1,0:T(8,128)(2,1)} async-done(((bf16[1792,640]{1,0:T(8,128)(2,1)}), bf16[448,640]{1,0:T(8,128)(2,1)}) %reduce-scatter.8.cloned.1.call-update) | async-done | bytes 573456 | tf_op jit(solution)/shard_map/reduce_scatter | solution.py:24
  372.3 0.0 copy-done
  372.3 0.0 copy-done.1
  372.3 2.2 multiply_convert_fusion
Async XLA Ops:
  6.5 41.5 %all-gather.5.cloned.1.call-start = ((), (), s32[]{:S(2)}) async-start(), calls=%async_computation.3 | async-start | bytes 2867200 | tf_op jit(solution)/shard_map/all_gather | solution.py:14
  7.3 96.5 %all-gather.7.cloned.1.call-start = ((), (), s32[]{:S(2)}) async-start(), calls=%async_computation.4 | async-start | bytes 2867200 | tf_op jit(solution)/shard_map/all_gather | solution.py:15
  8.0 174.2 %reduce-scatter.4.cloned.1.call-start = ((), (), s32[]{:S(2)}) async-start(), calls=%async_computation.5 | async-start | bytes 6823936 | tf_op jit(solution)/shard_map/reduce_scatter | solution.py:19
  112.8 118.7 %copy-start.2 = (bf16[1792,640]{1,0:T(8,128)(2,1)S(1)}, bf16[1792,640]{1,0:T(8,128)(2,1)}, u32[]{:S(2)}) copy-start(bf16[1792,640]{1,0:T(8,128)(2,1)} %all-gather.7.cloned.1.call-done) | copy-start | bytes 6881284
  112.9 118.7 %all-gather.9.cloned.1.call-start = ((), (), s32[]{:S(2)}) async-start(), calls=%async_computation.6 | async-start | bytes 6823936 | tf_op jit(solution)/shard_map/all_gather | solution.py:20
  182.2 92.2 %reduce-scatter.6.cloned.1.call-start = ((), (), s32[]{:S(2)}) async-start(), calls=%async_computation.7 | async-start | bytes 2867200 | tf_op jit(solution)/shard_map/reduce_scatter | solution.py:24
  239.9 89.8 %all-gather.11.cloned.1.call-start = ((), (), s32[]{:S(2)}) async-start(), calls=%async_computation.8 | async-start | bytes 2867200 | tf_op jit(solution)/shard_map/all_gather | solution.py:27
  274.5 97.8 %reduce-scatter.8.cloned.1.call-start = ((), (), s32[]{:S(2)}) async-start(), calls=%async_computation.9 | async-start | bytes 2867200 | tf_op jit(solution)/shard_map/reduce_scatter | solution.py:24
  338.8 33.5 %copy-start = (bf16[448,640]{1,0:T(8,128)(2,1)S(1)}, bf16[448,640]{1,0:T(8,128)(2,1)}, u32[]{:S(2)}) copy-start(bf16[448,640]{1,0:T(8,128)(2,1)} %param.1) | copy-start | bytes 1720324
  338.8 33.5 %copy-start.1 = (bf16[448,640]{1,0:T(8,128)(2,1)S(1)}, bf16[448,640]{1,0:T(8,128)(2,1)}, u32[]{:S(2)}) copy-start(bf16[448,640]{1,0:T(8,128)(2,1)} %reduce-scatter.6.cloned.1.call-done) | copy-start | bytes 1720324
Sparse Core Ops, SparseCore 0:
  9.2 38.8 all-gather.4
  49.8 53.8 all-gather.6
  113.0 69.1 reduce-scatter.3
  183.9 47.5 all-gather.8
  240.1 34.3 reduce-scatter.5
  276.2 53.4 all-gather.10
  339.0 33.3 reduce-scatter.7

commit v2 on v1

v2 whole, which is shorter than its diff:
```python
import functools
import math

import jax
import jax.numpy as jnp
from jax import lax
from jax.experimental import pallas as pl
from jax.experimental.pallas import tpu as pltpu
from jax.sharding import Mesh, PartitionSpec as P

F32 = jnp.float32
BF16 = jnp.bfloat16
MESH = pl.DeviceIdType.MESH

N = 10240
R = 448
C = 640
J_CUTS = ((0, 384), (384, 512), (896, 384), (1280, 512))
C_CUTS = ((0, 256), (256, 256), (512, 128))
SIZE = {"zh": 4, "y": 4, "zl": 2, "x": 4, "core": 2}
PEERS = (("y", 1), ("y", -1), ("zh", 1), ("zh", -1), ("x", 1), ("x", -1), ("zl", 1), ("core", 1))
COPIES = 120


def dot_nt(a, b):
    return lax.dot_general(a, b, (((1,), (1,)), ((), ())), preferred_element_type=F32)


def dot(a, b):
    return jnp.dot(a, b, preferred_element_type=F32)


def kernel(
    x_ref, o_ref, rows_i, rows_j, gram, half_out, half_in, half, half_f32, rs1, rs2, own_f32, zl_out,
    zl_in, acc, yp, y1, y2, applied, yj, tp, t1, t2, t0, local_sem, send_sem, recv_sem,
):
    where = {name: lax.axis_index(name) for name in SIZE}
    core, x, zl = where["core"], where["x"], where["zl"]
    peer = {
        (name, step): {name: lax.rem(where[name] + step + SIZE[name], SIZE[name])}
        for name, step in PEERS
    }
    x_left, x_right, x_far = (lax.rem(x + d, 4) for d in (3, 1, 2))
    sent = []

    def send(src, dst, name, step):
        at = len(sent)
        copy = pltpu.make_async_remote_copy(
            src, dst, send_sem.at[at], recv_sem.at[at],
            device_id=peer[name, step], device_id_type=MESH,
        )
        copy.start()
        sent.append(copy)
        return copy

    local = [
        pltpu.make_async_copy(x_ref, rows_i.at[0], local_sem.at[0]),
        pltpu.make_async_copy(x_ref, rows_j.at[pl.ds(0, R)], local_sem.at[1]),
    ]
    for copy in local:
        copy.start()
    barrier = pltpu.get_barrier_semaphore()
    for name, step in PEERS:
        pl.semaphore_signal(barrier, inc=1, device_id=peer[name, step], device_id_type=MESH)
    pl.semaphore_wait(barrier, len(PEERS))
    for copy in local:
        copy.wait()

    def part(place, side=None):
        if side is None:
            return pl.ds(place * R, R)
        return pl.ds(place * R + side * (R // 2), R // 2)

    def gather_near(buf):
        return (
            send(buf.at[part(0)], buf.at[part(1)], "zh", -1),
            send(buf.at[part(0)], buf.at[part(2)], "zh", 1),
        )

    def gather_far(buf):
        return (
            send(buf.at[part(1, 0)], buf.at[part(3, 0)], "zh", -1),
            send(buf.at[part(2, 1)], buf.at[part(3, 1)], "zh", 1),
        )

    def arrive(copies):
        for copy in copies:
            copy.wait_recv()

    y_near = (
        send(rows_i.at[0], rows_i.at[1], "y", -1),
        send(rows_i.at[0], rows_i.at[2], "y", 1),
    )
    z_near = gather_near(rows_j)
    arrive(y_near)
    lo, hi = pl.ds(0, R // 2), pl.ds(R // 2, R // 2)
    y_far = (
        send(rows_i.at[1, lo], rows_i.at[3, lo], "y", -1),
        send(rows_i.at[2, hi], rows_i.at[3, hi], "y", 1),
    )

    flight = {}

    def products(j):
        if j == 0:
            arrive(y_far)
        elif j == 1:
            arrive(z_near)
            flight["z_far"] = gather_far(rows_j)
        elif j == 3:
            arrive(flight["z_far"])
        start, width = J_CUTS[j]

        def tile(place):
            return dot_nt(rows_i[place], rows_j[pl.ds(start, width)])

        def other(i, carry):
            half_out[j][pl.ds(2 * i, 2)] = tile(2 * (1 - core) + i).astype(BF16).reshape(2, 224, width)
            return carry

        def mine(i, carry):
            half_f32[pl.ds(2 * i, 2), :, :width] = tile(2 * core + i).reshape(2, 224, width)
            return carry

        lax.fori_loop(0, 2, other, 0)
        flight["core", j] = (send(half_out[j], half_in[j], "core", 1),)
        lax.fori_loop(0, 2, mine, 0)

    def pair_sum(j):
        width = J_CUTS[j][1]
        arrive(flight["core", j])

        def add(i, carry):
            half[j][i] = (half_f32[i, :, :width] + half_in[j][i].astype(F32)).astype(BF16)
            return carry

        lax.fori_loop(0, 4, add, 0)
        flight["rs1", j] = (
            send(half[j].at[x_far, pl.ds(0, 112)], rs1[j].at[0], "x", 1),
            send(half[j].at[x_far, pl.ds(112, 112)], rs1[j].at[1], "x", -1),
        )

    def ring_sum(j):
        for side, to, step in ((0, x_right, 1), (1, x_left, -1)):
            arrive(flight["rs1", j][side : side + 1])
            at = pl.ds(112 * side, 112)
            half[j][to, at] = (half[j][to, at].astype(F32) + rs1[j][side].astype(F32)).astype(BF16)
            flight["rs2", j, side] = send(half[j].at[to], rs2[j].at[side], "x", step)

    def own_sum(j):
        width = J_CUTS[j][1]
        arrive((flight["rs2", j, 0], flight["rs2", j, 1]))

        def total(side):
            at = pl.ds(pl.multiple_of(112 * side, 16), 112)
            return half[j][x, at].astype(F32) + rs2[j][0, at].astype(F32) + rs2[j][1, at].astype(F32)

        zl_out[j][...] = total(1 - zl).astype(BF16)
        flight["zl", j] = (send(zl_out[j], zl_in[j], "zl", 1),)
        own_f32[j][...] = total(zl)

    def piece(x_at, zl_at):
        return core * 8 + x_at * 2 + zl_at

    def settle(j):
        arrive(flight["zl", j])
        at = piece(x, zl)
        gram[j][at] = (own_f32[j][...] + zl_in[j][...].astype(F32)).astype(BF16)
        flight["zl_gather", j] = (send(gram[j].at[at], gram[j].at[at], "zl", 1),)

    def share(j, at):
        flight.setdefault(("share", j), []).append(send(at, at, "core", 1))

    def spread(j):
        arrive(flight["zl_gather", j])
        mine = gram[j].at[pl.ds(piece(x, 0), 2)]
        flight["near", j] = (send(mine, mine, "x", 1), send(mine, mine, "x", -1))
        share(j, mine)

    def forward(j):
        arrive(flight["near", j])
        left, right = gram[j].at[piece(x_left, 0)], gram[j].at[piece(x_right, 1)]
        flight["far", j] = (send(left, left, "x", 1), send(right, right, "x", -1))
        share(j, gram[j].at[pl.ds(piece(x_left, 0), 2)])
        share(j, gram[j].at[pl.ds(piece(x_right, 0), 2)])

    def finish(j):
        arrive(flight["far", j])
        share(j, gram[j].at[pl.ds(piece(x_far, 0), 2)])

    def gram_tile(j, place):
        return gram[j][pl.ds(4 * place, 4)].reshape(R, J_CUTS[j][1])

    def apply(j):
        arrive(flight["share", j])
        if j == 3:
            return
        start, width = J_CUTS[j]

        def one(place, carry):
            value = dot(gram_tile(j, place), rows_j[pl.ds(start, width)])
            acc[place] = value if j == 0 else acc[place] + value
            return carry

        lax.fori_loop(0, 4, one, 0)

    stages = (products, pair_sum, ring_sum, own_sum, settle, spread, forward, finish, apply)
    for tick in range(len(stages) + 3):
        for j in range(4):
            if 0 <= tick - j < len(stages):
                stages[tick - j](j)

    def scatter_far(buf, land):
        return (
            send(buf.at[2, lo], land.at[0], "y", 1),
            send(buf.at[2, hi], land.at[1], "y", -1),
        )

    def scatter_near(buf, land, landed, copies):
        out = []
        for side, at, to, step in ((0, lo, 0, 1), (1, hi, 1, -1)):
            arrive(copies[side : side + 1])
            buf[to, at] = (buf[to, at].astype(F32) + land[side].astype(F32)).astype(BF16)
            out.append(send(buf.at[to], landed.at[side], "y", step))
        return out

    def first(c):
        at, width = C_CUTS[c]
        cols = pl.ds(at, width)
        start, depth = J_CUTS[3]

        def value(place):
            return acc[place, :, cols] + dot(gram_tile(3, place), rows_j[pl.ds(start, depth), cols])

        yp[c][2] = value(3).astype(BF16)
        flight["y1", c] = scatter_far(yp[c], y1[c])
        yp[c][0] = value(1).astype(BF16)
        yp[c][1] = value(2).astype(BF16)
        applied[c][...] = value(0)

    def second(c):
        flight["y2", c] = scatter_near(yp[c], y1[c], y2[c], flight["y1", c])

    def third(c):
        arrive(flight["y2", c])
        value = applied[c][...] + y2[c][0].astype(F32) + y2[c][1].astype(F32)
        yj[c][pl.ds(0, R)] = value.astype(BF16)
        flight["yz", c] = gather_near(yj[c])
        applied[c][...] = value

    def fourth(c):
        arrive(flight["yz", c])
        flight["yf", c] = gather_far(yj[c])

    def fifth(c):
        arrive(flight["yf", c])

        def value(place):
            return sum(
                dot(gram_tile(j, place), yj[c][pl.ds(start, depth)])
                for j, (start, depth) in enumerate(J_CUTS)
            )

        tp[c][2] = value(3).astype(BF16)
        flight["t1", c] = scatter_far(tp[c], t1[c])
        tp[c][0] = value(1).astype(BF16)
        tp[c][1] = value(2).astype(BF16)
        t0[c][...] = value(0)

    def sixth(c):
        flight["t2", c] = scatter_near(tp[c], t1[c], t2[c], flight["t1", c])

    def seventh(c):
        arrive(flight["t2", c])
        at, width = C_CUTS[c]
        cols = pl.ds(at, width)
        twice = t0[c][...] + t2[c][0].astype(F32) + t2[c][1].astype(F32)
        total = 3.4445 * rows_i[0, :, cols].astype(F32) - 4.775 * applied[c][...] + 2.0315 * twice
        o_ref[:, cols] = (math.sqrt(N) * total).astype(BF16)

    steps = (first, second, third, fourth, fifth, sixth, seventh)
    for tick in range(len(steps) + 2):
        for c in range(3):
            if 0 <= tick - c < len(steps):
                steps[tick - c](c)

    for copy in sent:
        copy.wait_send()


def local(iterate):
    def per_chunk(*shape, dtype=BF16):
        return [pltpu.VMEM((*shape, width), dtype) for _, width in J_CUTS]

    def per_cut(*shape, dtype=BF16):
        return [pltpu.VMEM((*shape, width), dtype) for _, width in C_CUTS]

    scratch = dict(
        rows_i=pltpu.VMEM((4, R, C), BF16),
        rows_j=pltpu.VMEM((4 * R, C), BF16),
        gram=per_chunk(16, 112),
        half_out=per_chunk(4, 224),
        half_in=per_chunk(4, 224),
        half=per_chunk(4, 224),
        half_f32=pltpu.VMEM((4, 224, 512), F32),
        rs1=per_chunk(2, 112),
        rs2=per_chunk(2, 224),
        own_f32=per_chunk(112, dtype=F32),
        zl_out=per_chunk(112),
        zl_in=per_chunk(112),
        acc=pltpu.VMEM((4, R, C), F32),
        yp=per_cut(3, R),
        y1=per_cut(2, R // 2),
        y2=per_cut(2, R),
        applied=per_cut(R, dtype=F32),
        yj=per_cut(4 * R),
        tp=per_cut(3, R),
        t1=per_cut(2, R // 2),
        t2=per_cut(2, R),
        t0=per_cut(R, dtype=F32),
        local_sem=pltpu.SemaphoreType.DMA((2,)),
        send_sem=pltpu.SemaphoreType.DMA((COPIES,)),
        recv_sem=pltpu.SemaphoreType.DMA((COPIES,)),
    )
    return pl.pallas_call(
        kernel,
        out_shape=jax.ShapeDtypeStruct((R, C), BF16),
        in_specs=[pl.BlockSpec(memory_space=pl.ANY)],
        out_specs=pl.BlockSpec(memory_space=pltpu.VMEM),
        scratch_shapes=scratch,
        compiler_params=pltpu.CompilerParams(
            collective_id=0, has_side_effects=True, vmem_limit_bytes=60 * 2**20
        ),
        cost_estimate=pl.CostEstimate(
            flops=12_600_000_000, bytes_accessed=1_200_000, transcendentals=0
        ),
    )(iterate)


def solution(mesh):
    fine = Mesh(mesh.devices.reshape(4, 4, 2, 4, 2), tuple(SIZE))
    spec = P(("zh", "y"), ("zl", "x", "core"))
    return jax.shard_map(local, mesh=fine, in_specs=(spec,), out_specs=spec, check_vma=False)
```

time: 382 us -> 180 us (0.47)
  waiting for transfers between devices: 339 us -> 0 us
  Pallas kernels: 0 us -> 178 us
  matrix products: 26.5 us -> 0 us
  between operations: 13.5 us -> 0.01 us
    all_gather x4 -> x0, waiting for transfers between devices: 200 us -> none  [the longest x1 55.7 us: local(): rows_j = lax.all_gather(iterate, 'zh', axis=0, tiled=True)]
    pallas_call x0 -> x1, Pallas kernels: none -> 178 us  [local(): pl.pallas_call(kernel, out_shape=jax.ShapeDtypeStruct((R, C), BF16), in_s...]
    reduce_scatter x3 -> x0, waiting for transfers between devices: 137 us -> none  [the longest x1 69.3 us: local(): lax.psum_scatter(part, ('zl', 'x', 'core'), scatter_dimension=0, tiled=True)]
    dot_general x3 -> x0, matrix products: 26.5 us -> none  [the longest x2 17.4 us: apply(): out = jnp.dot(gram, right, preferred_element_type=F32).astype(BF16)]
  transfers between devices with their start and end apart: 7 -> 0, of which waited for: 7 -> 0; matrix products, arithmetic and copies ran while one was open for 0% -> 0% of each run, Pallas kernels for 0% -> 0%
where the time goes in v2:
time: 180 us
  Pallas kernels  178 us (99%)
  local copies, waits for them, and re-layouts  1.92 us (1%)
    pallas_call x1, Pallas kernels, local(): pl.pallas_call(kernel, out_shape=jax.ShapeDtypeStruct((R, C), BF16), in_s...  178 us

profile of v2, /device:TPU:1, one launch (start us, length us, event | category | flops | bytes accessed | tf_op | source)
XLA Modules:
  0.0 179.9 jit_solution(12503460917403082261)
XLA Ops:
  0.0 178.0 %shard_map.17 = bf16[448,640]{1,0:T(8,128)(2,1)} custom-call(bf16[448,640]{1,0:T(8,128)(2,1)} %x_ref.1), custom_call_target="tpu_custom_call" | custom-call | flops 12600000512 | bytes 1200000 | tf_op jit(solution)/shard_map/pallas_call | solution.py:325
  178.0 1.9 %copy.3 = bf16[448,640]{1,0:T(8,128)(2,1)} copy(bf16[448,640]{1,0:T(8,128)(2,1)} %shard_map.17) | data formatting | bytes 1146880

commit v3 on v2

--- a/solution.py
+++ b/solution.py
@@ -16,10 +16,14 @@
 R = 448
 C = 640
 J_CUTS = ((0, 384), (384, 512), (896, 384), (1280, 512))
-C_CUTS = ((0, 256), (256, 256), (512, 128))
+C_CUTS = ((0, 128), (128, 128), (256, 128), (384, 128), (512, 128))
 SIZE = {"zh": 4, "y": 4, "zl": 2, "x": 4, "core": 2}
 PEERS = (("y", 1), ("y", -1), ("zh", 1), ("zh", -1), ("x", 1), ("x", -1), ("zl", 1), ("core", 1))
-COPIES = 120
+COPIES = 160
+READY = (27, 38, 40, 53)
+STEP = 7
+TIMES = (0, 3, 6, 16, 23, 27, 31)
+PACE = (2, 2, 2.5, 6, 7, 7, 7)
 
 
 def dot_nt(a, b):
@@ -119,7 +123,7 @@
             return carry
 
         def mine(i, carry):
-            half_f32[pl.ds(2 * i, 2), :, :width] = tile(2 * core + i).reshape(2, 224, width)
+            half_f32[j][pl.ds(2 * i, 2)] = tile(2 * core + i).reshape(2, 224, width)
             return carry
 
         lax.fori_loop(0, 2, other, 0)
@@ -131,7 +135,7 @@
         arrive(flight["core", j])
 
         def add(i, carry):
-            half[j][i] = (half_f32[i, :, :width] + half_in[j][i].astype(F32)).astype(BF16)
+            half[j][i] = (half_f32[j][i] + half_in[j][i].astype(F32)).astype(BF16)
             return carry
 
         lax.fori_loop(0, 4, add, 0)
@@ -205,10 +209,10 @@
         lax.fori_loop(0, 4, one, 0)
 
     stages = (products, pair_sum, ring_sum, own_sum, settle, spread, forward, finish, apply)
-    for tick in range(len(stages) + 3):
-        for j in range(4):
-            if 0 <= tick - j < len(stages):
-                stages[tick - j](j)
+    for _, j, stage in sorted(
+        (READY[j] + STEP * stage, j, stage) for j in range(len(J_CUTS)) for stage in range(len(stages))
+    ):
+        stages[stage](j)
 
     def scatter_far(buf, land):
         return (
@@ -279,10 +283,10 @@
         o_ref[:, cols] = (math.sqrt(N) * total).astype(BF16)
 
     steps = (first, second, third, fourth, fifth, sixth, seventh)
-    for tick in range(len(steps) + 2):
-        for c in range(3):
-            if 0 <= tick - c < len(steps):
-                steps[tick - c](c)
+    for _, c, step in sorted(
+        (TIMES[step] + PACE[step] * c, c, step) for c in range(len(C_CUTS)) for step in range(len(steps))
+    ):
+        steps[step](c)
 
     for copy in sent:
         copy.wait_send()
@@ -302,7 +306,7 @@
         half_out=per_chunk(4, 224),
         half_in=per_chunk(4, 224),
         half=per_chunk(4, 224),
-        half_f32=pltpu.VMEM((4, 224, 512), F32),
+        half_f32=per_chunk(4, 224, dtype=F32),
         rs1=per_chunk(2, 112),
         rs2=per_chunk(2, 224),
         own_f32=per_chunk(112, dtype=F32),

time: 180 us -> 168 us (0.933)
  the two profiles are of different devices: /device:TPU:1 before, /device:TPU:14 now
where the time goes in v3:
time: 168 us
  Pallas kernels  166 us (99%)
  local copies, waits for them, and re-layouts  1.92 us (1%)
    pallas_call x1, Pallas kernels, local(): pl.pallas_call(kernel, out_shape=jax.ShapeDtypeStruct((R, C), BF16), in_s...  166 us

profile of v3, /device:TPU:14, one launch (start us, length us, event | category | flops | bytes accessed | tf_op | source)
XLA Modules:
  0.0 167.6 jit_solution(2701625064241310574)
XLA Ops:
  0.0 165.7 %shard_map.17 = bf16[448,640]{1,0:T(8,128)(2,1)} custom-call(bf16[448,640]{1,0:T(8,128)(2,1)} %x_ref.1), custom_call_target="tpu_custom_call" | custom-call | flops 12600000512 | bytes 1200000 | tf_op jit(solution)/shard_map/pallas_call | solution.py:329
  165.7 1.9 %copy.3 = bf16[448,640]{1,0:T(8,128)(2,1)} copy(bf16[448,640]{1,0:T(8,128)(2,1)} %shard_map.17) | data formatting | bytes 1146880

commit v4 on v3

--- a/solution.py
+++ b/solution.py
@@ -20,6 +20,8 @@
 SIZE = {"zh": 4, "y": 4, "zl": 2, "x": 4, "core": 2}
 PEERS = (("y", 1), ("y", -1), ("zh", 1), ("zh", -1), ("x", 1), ("x", -1), ("zl", 1), ("core", 1))
 COPIES = 160
+PAIR_FIRST = (2,)
+TOP, LOW = pl.ds(0, 64), pl.ds(64, 48)
 READY = (27, 38, 40, 53)
 STEP = 7
 TIMES = (0, 3, 6, 16, 23, 27, 31)
@@ -36,7 +38,7 @@
 
 def kernel(
     x_ref, o_ref, rows_i, rows_j, gram, half_out, half_in, half, half_f32, rs1, rs2, own_f32, zl_out,
-    zl_in, acc, yp, y1, y2, applied, yj, tp, t1, t2, t0, local_sem, send_sem, recv_sem,
+    zl_in, pair_in, pair, acc, yp, y1, y2, applied, yj, tp, t1, t2, t0, local_sem, send_sem, recv_sem,
 ):
     where = {name: lax.axis_index(name) for name in SIZE}
     core, x, zl = where["core"], where["x"], where["zl"]
@@ -139,6 +141,10 @@
             return carry
 
         lax.fori_loop(0, 4, add, 0)
+        if j in PAIR_FIRST:
+            theirs = pl.ds(pl.multiple_of(112 * (1 - zl), 16), 112)
+            flight["zl", j] = (send(half[j].at[:, theirs], pair_in[j], "zl", 1),)
+            return
         flight["rs1", j] = (
             send(half[j].at[x_far, pl.ds(0, 112)], rs1[j].at[0], "x", 1),
             send(half[j].at[x_far, pl.ds(112, 112)], rs1[j].at[1], "x", -1),
@@ -208,11 +214,62 @@
 
         lax.fori_loop(0, 4, one, 0)
 
+    def pair_ring(j):
+        arrive(flight["zl", j])
+        ours = pl.ds(pl.multiple_of(112 * zl, 16), 112)
+        for i in range(4):
+            pair[j][i] = (half[j][i, ours].astype(F32) + pair_in[j][i].astype(F32)).astype(BF16)
+        flight["rs1", j] = (
+            send(pair[j].at[x_far, TOP], rs1[j].at[0, TOP], "x", 1),
+            send(pair[j].at[x_far, LOW], rs1[j].at[1, LOW], "x", -1),
+        )
+
+    def pair_ring_sum(j):
+        for side, to, at, step in ((0, x_right, TOP, 1), (1, x_left, LOW, -1)):
+            arrive(flight["rs1", j][side : side + 1])
+            pair[j][to, at] = (pair[j][to, at].astype(F32) + rs1[j][side, at].astype(F32)).astype(BF16)
+            flight["rs2", j, side] = send(pair[j].at[to], rs2[j].at[side, pl.ds(0, 112)], "x", step)
+
+    def pair_share(j, x_at):
+        at = gram[j].at[piece(x_at, zl)]
+        flight.setdefault(("pair", j), []).append((x_at, send(at, at, "zl", 1)))
+        share(j, at)
+
+    def pair_settle(j):
+        arrive((flight["rs2", j, 0], flight["rs2", j, 1]))
+        mine = gram[j].at[piece(x, zl)]
+        rest = pl.ds(0, 112)
+        mine[...] = (
+            pair[j][x].astype(F32) + rs2[j][0, rest].astype(F32) + rs2[j][1, rest].astype(F32)
+        ).astype(BF16)
+        flight["near", j] = (send(mine, mine, "x", 1), send(mine, mine, "x", -1))
+        pair_share(j, x)
+
+    def pair_forward(j):
+        arrive(flight["near", j])
+        left, right = gram[j].at[piece(x_left, zl), TOP], gram[j].at[piece(x_right, zl), LOW]
+        flight["far", j] = (send(left, left, "x", 1), send(right, right, "x", -1))
+        pair_share(j, x_left)
+        pair_share(j, x_right)
+
+    def pair_finish(j):
+        arrive(flight["far", j])
+        pair_share(j, x_far)
+
+    def pair_spread(j):
+        for x_at, copy in flight["pair", j]:
+            arrive((copy,))
+            share(j, gram[j].at[piece(x_at, 1 - zl)])
+
+    pair_stages = (
+        products, pair_sum, pair_ring, pair_ring_sum, pair_settle, pair_forward, pair_finish,
+        pair_spread, apply,
+    )
     stages = (products, pair_sum, ring_sum, own_sum, settle, spread, forward, finish, apply)
     for _, j, stage in sorted(
         (READY[j] + STEP * stage, j, stage) for j in range(len(J_CUTS)) for stage in range(len(stages))
     ):
-        stages[stage](j)
+        (pair_stages if j in PAIR_FIRST else stages)[stage](j)
 
     def scatter_far(buf, land):
         return (
@@ -312,6 +369,8 @@
         own_f32=per_chunk(112, dtype=F32),
         zl_out=per_chunk(112),
         zl_in=per_chunk(112),
+        pair_in=per_chunk(4, 112),
+        pair=per_chunk(4, 112),
         acc=pltpu.VMEM((4, R, C), F32),
         yp=per_cut(3, R),
         y1=per_cut(2, R // 2),

time: 168 us -> 169 us (level)
  the two profiles are of different devices: /device:TPU:14 before, /device:TPU:1 now
where the time goes in v4:
time: 169 us; the launch traced here: 168 us
  Pallas kernels  166 us (98%)
  local copies, waits for them, and re-layouts  1.92 us (1%)
    pallas_call x1, Pallas kernels, local(): pl.pallas_call(kernel, out_shape=jax.ShapeDtypeStruct((R, C), BF16), in_s...  166 us

profile of v4, /device:TPU:1, one launch (start us, length us, event | category | flops | bytes accessed | tf_op | source)
XLA Modules:
  0.0 168.3 jit_solution(12474823653998332345)
XLA Ops:
  0.0 166.3 %shard_map.17 = bf16[448,640]{1,0:T(8,128)(2,1)} custom-call(bf16[448,640]{1,0:T(8,128)(2,1)} %x_ref.1), custom_call_target="tpu_custom_call" | custom-call | flops 12600000512 | bytes 1200000 | tf_op jit(solution)/shard_map/pallas_call | solution.py:388
  166.3 1.9 %copy.3 = bf16[448,640]{1,0:T(8,128)(2,1)} copy(bf16[448,640]{1,0:T(8,128)(2,1)} %shard_map.17) | data formatting | bytes 1146880
